TPU v7x, 32 devices: a whole 2x2x4 slice. The times are simulated.
32 devices in a mesh: ctx: 8 (over z, y), tp: 4 (over x, core).
Axes of the slice: x: 2, y: 2, z: 4, core: 2. Of those that a mesh axis runs over, the one named last changes fastest.
Arguments:
- block_q: bfloat16 [2048, 8192], P('ctx', 'tp'), may hold values from -200 to 200
- block_kv: bfloat16 [2, 2048, 1024], P(None, 'ctx', 'tp'), may hold values from -6 to 6
- lengths: int32 [8], P('ctx'), may hold values from 128 to 256, as said below
- tenant: int32 [1], replicated, may hold values from 0 to 7
- prefix_kv: bfloat16 [2, 8, 512, 1024], P(None, 'ctx', None, 'tp'), may hold values from -6 to 6
- decode_q: bfloat16 [2, 8, 8192], P(None, 'ctx', 'tp'), may hold values from -200 to 200
- decode_pos: int32 [2, 8], P(None, 'ctx'), may hold values from 513 to 2048
Outputs:
- prefill_out: bfloat16 [2048, 8192], P('ctx', 'tp')
- decode_out: bfloat16 [2, 8, 8192], P(None, 'ctx', 'tp')
Inputs may be any that keep to these rules, and one draw needn't show every extreme that they name: The lengths sum to 1536.
All inputs are finite; a program needn't handle non-finite values.
Results may differ from a plain program's by a relative error of at most 0.007.
Values may be sent and summed in bfloat16 or wider, within the bound.
A program may use at most 320 MiB of HBM per device.

v0:
```python
import jax
import jax.numpy as jnp
from jax import lax
from jax.sharding import PartitionSpec as P

HD = 128


MASKED_SCORE = -1e30


def broadcast(value, axis, source):
    kept = jnp.where(lax.axis_index(axis) == source, value, 0).astype(value.dtype)
    return lax.psum(kept, axis)


def carried_in(value, axis, join, neutral):
    count, mine = (lax.axis_size(axis), lax.axis_index(axis))
    pieces = lax.all_gather(value, axis)
    total = jnp.full_like(value, 0) + jnp.asarray(neutral, value.dtype)

    def hop(position, total):
        longer = join(total, pieces[position])
        return jnp.where(position < mine, longer, total)

    return lax.fori_loop(0, count - 1, hop, total)


def joined(value, axis, join):
    pieces = jax.tree.map(lambda part: lax.all_gather(part, axis), value)
    head = jax.tree.map(lambda part: part[0], pieces)
    tail = jax.tree.map(lambda part: part[1:], pieces)
    total, _ = lax.scan(lambda total, section: (join(total, section), None), head, tail)
    return total


def attend(queries, key_rows, value_rows, visible):
    scale = HD ** (-0.5)
    scores = (
        jnp.einsum("rgd,kd->rgk", queries, key_rows, preferred_element_type=jnp.float32) * scale
    )
    allowed = visible[:, None, :]
    highest = jnp.max(jnp.where(allowed, scores, MASKED_SCORE), axis=-1)
    weights = jnp.where(allowed, jnp.exp(scores - highest[..., None]), 0.0)
    weight_sum = jnp.sum(weights, axis=-1)
    weighted = jnp.einsum(
        "rgk,kd->rgd", weights.astype(jnp.bfloat16), value_rows, preferred_element_type=jnp.float32
    )
    return (highest, weight_sum, weighted)


def combine(first, second):
    highest = jnp.maximum(first[0], second[0])
    first_scale = jnp.exp(first[0] - highest)
    second_scale = jnp.exp(second[0] - highest)
    weight_sum = first[1] * first_scale + second[1] * second_scale
    shape = first[0].shape + (-1,)
    weighted = (
        first[2].reshape(shape) * first_scale[..., None]
        + second[2].reshape(shape) * second_scale[..., None]
    )
    return (highest, weight_sum, weighted.reshape(first[2].shape))


def add_counts(earlier, later):
    return earlier + later


def body(block_q, block_kv, lengths, tenant, prefix_kv, decode_q, decode_pos):
    row_count = block_q.shape[0]
    head_count = block_q.shape[1] // HD
    kv_heads = block_kv.shape[2] // HD
    group_size = head_count // kv_heads
    my_block = lax.axis_index("ctx")
    length = lengths[0]
    stored = prefix_kv[:, 0]
    anchor = broadcast(stored, "ctx", tenant[0])
    anchor_len = anchor.shape[1]
    key_rows = jnp.concatenate([anchor[0], block_kv[0]], 0).reshape(
        anchor_len + row_count, kv_heads, HD
    )
    value_rows = jnp.concatenate([anchor[1], block_kv[1]], 0).reshape(
        anchor_len + row_count, kv_heads, HD
    )
    token_index = jnp.arange(row_count, dtype=jnp.int32)
    key_index = jnp.arange(anchor_len + row_count, dtype=jnp.int32) - anchor_len
    visible = (key_index[None, :] < 0) | (key_index[None, :] <= token_index[:, None]) & (
        key_index[None, :] < length
    )
    head_queries = jnp.transpose(block_q.reshape(row_count, head_count, HD), (1, 0, 2))

    def one_head(element):
        queries, head_index = element
        kv_slot = head_index // group_size
        head_keys = lax.dynamic_index_in_dim(key_rows, kv_slot, 1, keepdims=False)
        head_values = lax.dynamic_index_in_dim(value_rows, kv_slot, 1, keepdims=False)
        highest, weight_sum, weighted = attend(queries[:, None, :], head_keys, head_values, visible)
        return weighted[:, 0, :] / weight_sum

    prefilled = lax.map(one_head, (head_queries, jnp.arange(head_count, dtype=jnp.int32)))
    prefilled = jnp.transpose(prefilled, (1, 0, 2)).reshape(row_count, head_count * HD)
    prefill_out = jnp.where(token_index[:, None] < length, prefilled, 0.0).astype(jnp.bfloat16)
    offset = carried_in(lengths, "ctx", add_counts, jnp.zeros_like(lengths))[0]
    queries_all, limits = (
        lax.all_gather(decode_q, "ctx", axis=1, tiled=True),
        lax.all_gather(decode_pos, "ctx", axis=1, tiled=True),
    )
    step_count, query_count = limits.shape
    flat_count = step_count * query_count
    flat_queries = queries_all.reshape(flat_count, kv_heads, group_size, HD)
    flat_limits = limits.reshape(flat_count)
    local_pos = (anchor_len + offset + token_index).astype(jnp.int32)
    local_ok = token_index < length

    def block_partial(key_block, value_block, key_pos, key_ok):
        seen = key_ok[None, :] & (key_pos[None, :] < flat_limits[:, None])
        key_heads = key_block.reshape(-1, kv_heads, HD)
        value_heads = value_block.reshape(-1, kv_heads, HD)
        partials = [
            attend(
                flat_queries[:, slot_index],
                key_heads[:, slot_index],
                value_heads[:, slot_index],
                seen,
            )
            for slot_index in range(kv_heads)
        ]
        highest = jnp.concatenate([item[0] for item in partials], 1)
        weight_sum = jnp.concatenate([item[1] for item in partials], 1)
        weighted = jnp.concatenate([item[2] for item in partials], 1)
        return (
            highest.reshape(step_count, query_count, head_count),
            weight_sum.reshape(step_count, query_count, head_count),
            weighted.reshape(step_count, query_count, head_count * HD),
        )

    local_part = block_partial(block_kv[0], block_kv[1], local_pos, local_ok)

    def with_prefix():
        return block_partial(
            stored[0],
            stored[1],
            jnp.arange(anchor_len, dtype=jnp.int32),
            jnp.ones((anchor_len,), dtype=bool),
        )

    def without_prefix():
        return (
            jnp.full((step_count, query_count, head_count), MASKED_SCORE, jnp.float32),
            jnp.zeros((step_count, query_count, head_count), jnp.float32),
            jnp.zeros((step_count, query_count, head_count * HD), jnp.float32),
        )

    prefix_part = lax.cond(my_block == tenant[0], with_prefix, without_prefix)
    result = combine(local_part, prefix_part)
    own_rows = query_count // lax.axis_size("ctx")
    merged = joined(result, "ctx", combine)
    weight_sum = lax.dynamic_slice_in_dim(merged[1], my_block * own_rows, own_rows, 1)
    weighted = lax.dynamic_slice_in_dim(merged[2], my_block * own_rows, own_rows, 1)
    decoded = weighted.reshape(step_count, own_rows, head_count, HD) / weight_sum[..., None]
    decode_out = decoded.reshape(step_count, own_rows, head_count * HD).astype(jnp.bfloat16)
    return (prefill_out, decode_out)


def solution(mesh):
    in_specs = (
        P("ctx", "tp"),
        P(None, "ctx", "tp"),
        P("ctx"),
        P(),
        P(None, "ctx", None, "tp"),
        P(None, "ctx", "tp"),
        P(None, "ctx"),
    )
    out_specs = (P("ctx", "tp"), P(None, "ctx", "tp"))
    return jax.shard_map(body, mesh=mesh, in_specs=in_specs, out_specs=out_specs, check_vma=False)
```

profile of v0, /device:TPU:0, one launch (start us, length us, event | category | flops | bytes accessed | tf_op | source)
XLA Modules:
  0.0 246.1 jit_solution(16555097412754607328)
XLA Ops:
  7.9 1.3 copy.77
  9.2 0.8 broadcast_select_fusion
  11.3 0.7 dynamic-update-slice
  12.0 13.1 %all-reduce = s32[8]{0:T(128)S(1)} all-reduce(s32[8]{0:T(128)S(1)} %dynamic-update-slice), channel_id=2, replica_groups=mesh['ctx'=8,'tp'=4] {'ctx'}, use_global_device_ids=true, to_apply=%add | all-reduce | flops 8 | bytes 64
  25.0 7.9 %while.40 = (s32[]{:T(128)}, s32[1]{0:T(128)}, s32[]{:T(128)}, s32[8,1]{0,1:T(1,128)S(1)}, s32[]{:T(128)}) while((s32[]{:T(128)}, s32[1]{0:T(128)}, s32[]{:T(128)}, s32[8,1]{0,1:T(1,128)S(1)}, s32[]{:T(128)}) %tuple.133), condition=%wide.region_6.7_spmd, body=%wide.region_5.6_spmd.sunk | while | flops 5 | bytes 107 | solution.py:26
  32.9 17.7 %all-gather.3 = s32[8,1,2]{2,1,0:T(1,128)S(1)} all-gather(s32[1,1,2]{2,1,0:T(1,128)S(1)} %bitcast.229), channel_id=1, replica_groups=mesh['ctx'=8,'tp'=4] {'ctx'}, dimensions={0}, use_global_device_ids=true | all-gather | bytes 72 | tf_op jit(solution)/shard_map/all_gather | solution.py:106
  50.9 30.6 %all_gather.30 = bf16[2,8,2048]{2,0,1:T(2,128)(2,1)S(1)} all-gather(bf16[2,1,2048]{2,0,1:T(2,128)(2,1)S(1)} %copy-done.5), channel_id=1, replica_groups=mesh['ctx'=8,'tp'=4] {'ctx'}, dimensions={1}, use_global_device_ids=true | all-gather | bytes 73728 | tf_op jit(solution)/shard_map/all_gather | solution.py:105
  83.2 0.8 fusion.43
  84.0 30.6 %all-gather.1 = f32[16,8,16]{2,1,0:T(8,128)S(1)} all-gather(f32[2,8,16]{2,1,0:T(8,128)S(1)} %get-tuple-element.339), channel_id=3, replica_groups=mesh['ctx'=8,'tp'=4] {'ctx'}, dimensions={0}, use_global_device_ids=true | all-gather | bytes 9216 | tf_op jit(solution)/shard_map/all_gather | solution.py:30
  114.6 30.6 %all-gather.2 = f32[16,8,16]{2,1,0:T(8,128)S(1)} all-gather(f32[2,8,16]{2,1,0:T(8,128)S(1)} %get-tuple-element.336), channel_id=4, replica_groups=mesh['ctx'=8,'tp'=4] {'ctx'}, dimensions={0}, use_global_device_ids=true | all-gather | bytes 9216 | tf_op jit(solution)/shard_map/all_gather | solution.py:30
  145.2 1.3 copy.76
  146.5 1.1 fusion.69
  147.7 85.5 %while.42 = (s32[]{:T(128)}, bf16[16,256,128]{2,1,0:T(8,128)(2,1)S(1)}, bf16[16,256,128]{1,2,0:T(8,128)(2,1)}, s32[16]{0:T(128)S(1)}, bf16[768,2,128]{0,2,1:T(8,...) while((s32[]{:T(128)}, ...), condition=%wide.region_4.5_spmd.clone, body=%wide.region_1.4_spmd.clone.sunk | while | flops 104234512 | bytes 2971997 | solution.py:100
  150.9 1.3 select_reduce_fusion.6
  156.2 1.3 select_reduce_fusion.6
  161.5 1.3 select_reduce_fusion.6
  166.9 1.3 select_reduce_fusion.6
  172.2 1.3 select_reduce_fusion.6
  177.6 1.3 select_reduce_fusion.6
  182.9 1.3 select_reduce_fusion.6
  188.2 1.3 select_reduce_fusion.6
  193.6 1.3 select_reduce_fusion.6
  198.9 1.3 select_reduce_fusion.6
  204.3 1.3 select_reduce_fusion.6
  209.6 1.3 select_reduce_fusion.6
  214.9 1.3 select_reduce_fusion.6
  220.3 1.3 select_reduce_fusion.6
  225.6 1.3 select_reduce_fusion.6
  231.0 1.3 select_reduce_fusion.6
  233.1 1.2 fusion.42
  234.4 1.2 copy-done
  235.9 2.5 %while.41 = (s32[]{:T(128)}, f32[2,8,16]{2,1,0:T(8,128)S(1)}, f32[2,8,16]{2,1,0:T(8,128)S(1)}, f32[2,8,2048]{2,1,0:T(8,128)S(1)}, f32[7,2,8,16]{3,2,1,0:T(8,128)...) while((s32[]{:T(128)}, f32[2,8,16]{2,1,0:T(8,128)S(1)}, ...), condition=%wide.region_18.19_spmd, body=%wide.region_17.18_spmd.sunk | while | flops 99842 | bytes 407645 | solution.py:33
  (150 shorter events, 32.7 us)
Async XLA Ops:
  7.2 139.3 %all-reduce.3.cloned.1.call-start = ((), (), s32[]{:S(2)}) async-start(), calls=%async_computation | async-start | bytes 1048576 | tf_op jit(solution)/shard_map/psum | solution.py:14
  9.1 1.6 copy-start.7
  9.1 23.8 %copy-start.6 = (s32[2,1]{0,1:T(1,128)S(1)}, s32[2,1]{0,1:T(1,128)}, u32[]{:S(2)}) copy-start(s32[2,1]{0,1:T(1,128)} %param.21) | copy-start | bytes 28
  9.1 41.6 %copy-start.4 = (bf16[2,256,256]{2,1,0:T(8,128)(2,1)S(1)}, bf16[2,256,256]{2,1,0:T(8,128)(2,1)}, u32[]{:S(2)}) copy-start(bf16[2,256,256]{2,1,0:T(8,128)(2,1)} %param.16) | copy-start | bytes 786436
  9.2 41.7 %copy-start.5 = (bf16[2,1,2048]{2,0,1:T(2,128)(2,1)S(1)}, bf16[2,1,2048]{2,0,1:T(2,128)(2,1)}, u32[]{:S(2)}) copy-start(bf16[2,1,2048]{2,0,1:T(2,128)(2,1)} %param.20) | copy-start | bytes 24580
  10.0 224.3 %all-gather.6.cloned.1.call-start = ((), (), s32[]{:S(2)}) async-start(), calls=%async_computation.1 | async-start | bytes 1179648 | tf_op jit(solution)/shard_map/all_gather | solution.py:30
  82.9 62.3 %copy-start.1 = (bf16[256,2048]{1,0:T(8,128)(2,1)S(1)}, bf16[256,2048]{1,0:T(8,128)(2,1)}, u32[]{:S(2)}) copy-start(bf16[256,2048]{1,0:T(8,128)(2,1)} %param.15) | copy-start | bytes 3145732
  114.5 33.1 %copy-start.3 = (f32[16,8,16]{2,1,0:T(8,128)}, f32[16,8,16]{2,1,0:T(8,128)S(1)}, u32[]{:S(2)}) copy-start(f32[16,8,16]{2,1,0:T(8,128)S(1)} %all-gather.1) | copy-start | bytes 24580
  145.1 2.5 %copy-start.2 = (f32[16,8,16]{2,1,0:T(8,128)}, f32[16,8,16]{2,1,0:T(8,128)S(1)}, u32[]{:S(2)}) copy-start(f32[16,8,16]{2,1,0:T(8,128)S(1)} %all-gather.2) | copy-start | bytes 24580
  234.3 1.3 slice-start.1
  234.3 1.3 slice-start.2
  234.4 1.2 copy-start
  234.4 1.5 slice-start
Sparse Core Ops, SparseCore 0:
  11.4 75.0 all-reduce.2
  88.9 39.5 all-gather.5
where the time goes:
time: 248 us; the launch traced here: 246 us
  blocking collectives  122 us (49%)
  loops' own time  46.2 us (19%)
  matrix products  28.4 us (11%)
  local copies, waits for them, and re-layouts  21.5 us (9%)
  between operations  15.6 us (6%)
  other arithmetic  11.7 us (5%)
    all_gather x2, blocking collectives, joined(): pieces = jax.tree.map(lambda part: lax.all_gather(part, axis), value)  61.1 us
    another operation x1, loops' own time, body(): lax.map(one_head, (head_queries, jnp.arange(head_count, dtype=jnp.int32)))  42.1 us
    all_gather x1, blocking collectives, body(): lax.all_gather(decode_q, 'ctx', axis=1, tiled=True)  30.6 us
    dot_general x18, matrix products, attend(): jnp.einsum('rgd,kd->rgk', queries, key_rows, preferred_element_type=jnp.f...  21.2 us
    all_gather x1, blocking collectives, body(): lax.all_gather(decode_pos, 'ctx', axis=1, tiled=True)  17.7 us
    unnamed x1, blocking collectives  13.1 us
    dynamic_slice x16, local copies, waits for them, and re-layouts, body(): lax.map(one_head, (head_queries, jnp.arange(head_count, dtype=jnp.int32)))  9.38 us
    dot_general x18, matrix products, attend(): jnp.einsum('rgk,kd->rgd', weights.astype(jnp.bfloat16), value_rows, prefe...  7.27 us
  transfers between devices with their start and end apart: 2, of which 0 were waited for; matrix products, arithmetic and copies ran while one was open for 22% of the time, Pallas kernels for 0%

commit v1 on v0

v1 whole, which is shorter than its diff:
```python
import functools
import math

import jax
import jax.numpy as jnp
from jax import lax
from jax.experimental import pallas as pl
from jax.experimental.pallas import tpu as pltpu
from jax.sharding import PartitionSpec as P

HD = 128
MASKED = -1e30
SCALE2 = HD ** (-0.5) * math.log2(math.e)
F32 = jnp.float32
BF16 = jnp.bfloat16


def scores_of(q, k):
    return lax.dot_general(q, k, (((1,), (1,)), ((), ())), preferred_element_type=F32)


def mix(p, v):
    return lax.dot_general(p.astype(BF16), v, (((1,), (0,)), ((), ())), preferred_element_type=F32)


def parts_of(x):
    high = x.astype(BF16)
    rest = x - high.astype(F32)
    middle = rest.astype(BF16)
    low = (rest - middle.astype(F32)).astype(BF16)
    return high.astype(F32), middle.astype(F32), low.astype(F32)


def kernel(
    n, len_ref, pos_ref, q_ref, kv_ref, anchor_ref, dq_ref, out_ref, dout_ref,
    qall, info, psend, precv, q_send, q_recv, i_send, i_recv, p_send, p_recv,
):
    me = lax.axis_index("ctx")
    rows, width = q_ref.shape
    anc = anchor_ref.shape[1]
    groups = kv_ref.shape[2] // HD
    per_group = width // HD // groups
    steps = pos_ref.shape[0]
    drows = steps * per_group
    total = groups * drows
    length = len_ref[0]

    def remote(buffer, slot, to_slot, send, recv, peer):
        return pltpu.make_async_remote_copy(
            src_ref=buffer.at[slot], dst_ref=buffer.at[to_slot],
            send_sem=send, recv_sem=recv,
            device_id={"ctx": peer}, device_id_type=pl.DeviceIdType.MESH,
        )

    def query_copies(peer, source):
        return (
            remote(qall, me, source, q_send.at[peer], q_recv.at[source], peer),
            remote(info, me, source, i_send.at[peer], i_recv.at[source], peer),
        )

    def partial_copy(peer, source):
        return pltpu.make_async_remote_copy(
            src_ref=psend.at[peer], dst_ref=precv.at[source],
            send_sem=p_send.at[peer], recv_sem=p_recv.at[source],
            device_id={"ctx": peer}, device_id_type=pl.DeviceIdType.MESH,
        )

    def peers(act):
        def step(d, carry):
            act(lax.rem(me + d, n))
            return carry
        lax.fori_loop(1, n, step, 0)

    barrier = pltpu.get_barrier_semaphore()
    peers(lambda peer: pl.semaphore_signal(
        barrier, inc=1, device_id={"ctx": peer}, device_id_type=pl.DeviceIdType.MESH))
    qall[me] = dq_ref[...]
    for s in range(steps):
        info[me, s * per_group:(s + 1) * per_group] = jnp.full((per_group, HD), pos_ref[s, 0], jnp.int32)
    info[me, drows:drows + 8] = jnp.full((8, HD), length, jnp.int32)
    pl.semaphore_wait(barrier, n - 1)

    def send_queries(peer):
        for copy in query_copies(peer, me):
            copy.start()

    peers(send_queries)

    row_index = lax.broadcasted_iota(jnp.int32, (rows, rows), 0)
    key_index = lax.broadcasted_iota(jnp.int32, (rows, rows), 1)
    visible = (key_index <= row_index) & (key_index < length)
    kept_row = lax.broadcasted_iota(jnp.int32, (rows, HD), 0) < length

    def prefill_group(g):
        lanes = slice(g * HD, (g + 1) * HD)

        def head(i, carry):
            column = pl.ds(pl.multiple_of((g * per_group + i) * HD, HD), HD)
            q = q_ref[:, column]
            s_a = scores_of(q, anchor_ref[0, :, lanes])
            s_b = jnp.where(visible, scores_of(q, kv_ref[0, :, lanes]), MASKED)
            top = jnp.maximum(
                jnp.max(s_a, axis=1, keepdims=True), jnp.max(s_b, axis=1, keepdims=True))
            w_a = jnp.exp2((s_a - top) * SCALE2)
            w_b = jnp.exp2((s_b - top) * SCALE2)
            weight = jnp.sum(w_a, axis=1, keepdims=True) + jnp.sum(w_b, axis=1, keepdims=True)
            o = mix(w_a, anchor_ref[1, :, lanes]) + mix(w_b, kv_ref[1, :, lanes])
            out_ref[:, column] = jnp.where(kept_row, o * (1.0 / weight), 0.0).astype(BF16)
            return carry

        lax.fori_loop(0, per_group, head, 0)

    prefill_group(0)

    def wait_queries(peer):
        for copy in query_copies(peer, peer):
            copy.wait_recv()

    peers(wait_queries)

    def add_length(source, sum_):
        return sum_ + jnp.where(source < me, info[source, drows:drows + 8], 0)

    offset = lax.fori_loop(0, n, add_length, jnp.zeros((8, HD), jnp.int32))[0:1]
    limit = jnp.minimum(info[:, 0:drows].reshape(n * drows, HD) - (anc + offset), length)
    lane = lax.broadcasted_iota(jnp.int32, (n * drows, HD), 1)
    for g in range(groups):
        lanes = slice(g * HD, (g + 1) * HD)
        q = qall[:, g * drows:(g + 1) * drows].reshape(n * drows, HD)
        s = scores_of(q, kv_ref[0, :, lanes])
        seen = jnp.concatenate([lane + c * HD < limit for c in range(rows // HD)], axis=1)
        s = jnp.where(seen, s, MASKED)
        top = jnp.max(s, axis=1, keepdims=True)
        w = jnp.where(seen, jnp.exp2((s - top) * SCALE2), 0.0)
        weight = jnp.sum(w, axis=1, keepdims=True)
        o = mix(w, kv_ref[1, :, lanes]) * (1.0 / jnp.maximum(weight, 1e-30))
        psend[:, g * drows:(g + 1) * drows] = o.astype(BF16).reshape(n, drows, HD)
        stats = jnp.zeros((n * drows, HD), F32)
        for place, part in enumerate(parts_of(top) + parts_of(weight)):
            stats = jnp.where(lane // 16 == place, part, stats)
        psend[:, total + g * drows:total + (g + 1) * drows] = stats.astype(BF16).reshape(n, drows, HD)
    precv[me] = psend[me]
    peers(lambda peer: partial_copy(peer, me).start())

    for g in range(1, groups):
        prefill_group(g)

    own_limit = info[me, 0:drows]
    own_lane = lax.broadcasted_iota(jnp.int32, (drows, HD), 1)
    anchored = []
    for g in range(groups):
        lanes = slice(g * HD, (g + 1) * HD)
        s = scores_of(dq_ref[g * drows:(g + 1) * drows], anchor_ref[0, :, lanes])
        seen = jnp.concatenate([own_lane + c * HD < own_limit for c in range(anc // HD)], axis=1)
        s = jnp.where(seen, s, MASKED)
        top = jnp.max(s, axis=1, keepdims=True)
        w = jnp.where(seen, jnp.exp2((s - top) * SCALE2), 0.0)
        anchored.append((top, jnp.sum(w, axis=1, keepdims=True), mix(w, anchor_ref[1, :, lanes])))

    peers(lambda peer: partial_copy(peer, peer).wait_recv())
    for g in range(groups):
        def join(source, state):
            top, weight, o = state
            part = precv[source, g * drows:(g + 1) * drows].astype(F32)
            stats = precv[source, total + g * drows:total + (g + 1) * drows].astype(F32)
            part_top = stats[:, 0:1] + stats[:, 16:17] + stats[:, 32:33]
            part_weight = stats[:, 48:49] + stats[:, 64:65] + stats[:, 80:81]
            new_top = jnp.maximum(top, part_top)
            old = jnp.exp2((top - new_top) * SCALE2)
            new = jnp.exp2((part_top - new_top) * SCALE2) * part_weight
            return new_top, weight * old + new, o * old + part * new

        top, weight, o = lax.fori_loop(0, n, join, anchored[g])
        dout_ref[g * drows:(g + 1) * drows] = (o * (1.0 / weight)).astype(BF16)

    def wait_sends(peer):
        for copy in query_copies(peer, me):
            copy.wait_send()
        partial_copy(peer, me).wait_send()

    peers(wait_sends)


def body(n, block_q, block_kv, lengths, tenant, prefix_kv, decode_q, decode_pos):
    rows, width = block_q.shape
    groups = block_kv.shape[2] // HD
    per_group = width // HD // groups
    steps = decode_q.shape[0]
    total = steps * width // HD
    mine = lax.axis_index("ctx") == tenant[0]
    anchor = lax.psum(jnp.where(mine, prefix_kv[:, 0], 0).astype(BF16), "ctx")
    dq = decode_q.reshape(steps, groups, per_group, HD).transpose(1, 0, 2, 3).reshape(total, HD)
    vmem = pl.BlockSpec(memory_space=pltpu.VMEM)
    smem = pl.BlockSpec(memory_space=pltpu.SMEM)
    heads = width // HD
    keys = anchor.shape[1] + rows
    out, dout = pl.pallas_call(
        functools.partial(kernel, n),
        out_shape=(
            jax.ShapeDtypeStruct((rows, width), BF16),
            jax.ShapeDtypeStruct((total, HD), BF16),
        ),
        in_specs=[smem, smem, vmem, vmem, vmem, vmem],
        out_specs=(vmem, vmem),
        scratch_shapes=[
            pltpu.VMEM((n, total, HD), BF16),
            pltpu.VMEM((n, steps * per_group + 8, HD), jnp.int32),
            pltpu.VMEM((n, 2 * total, HD), BF16),
            pltpu.VMEM((n, 2 * total, HD), BF16),
        ] + [pltpu.SemaphoreType.DMA((n,))] * 6,
        compiler_params=pltpu.CompilerParams(
            collective_id=0, has_side_effects=True, vmem_limit_bytes=40 * 1024 * 1024),
        cost_estimate=pl.CostEstimate(
            flops=4 * heads * rows * keys * HD, bytes_accessed=4 * rows * width,
            transcendentals=heads * rows * keys),
        name="star_attention",
    )(lengths, decode_pos, block_q, block_kv, anchor, dq)
    dout = dout.reshape(groups, steps, per_group, HD).transpose(1, 0, 2, 3)
    return out, dout.reshape(steps, 1, width)


def solution(mesh):
    in_specs = (
        P("ctx", "tp"),
        P(None, "ctx", "tp"),
        P("ctx"),
        P(),
        P(None, "ctx", None, "tp"),
        P(None, "ctx", "tp"),
        P(None, "ctx"),
    )
    out_specs = (P("ctx", "tp"), P(None, "ctx", "tp"))
    return jax.shard_map(
        functools.partial(body, mesh.shape["ctx"]),
        mesh=mesh, in_specs=in_specs, out_specs=out_specs, check_vma=False)
```

time: 248 us -> 116 us (0.47)
  blocking collectives: 122 us -> 0 us
  waiting for transfers between devices: 0.04 us -> 76.5 us
  loops' own time: 46.2 us -> 0 us
  matrix products: 28.4 us -> 0 us
  local copies, waits for them, and re-layouts: 21.5 us -> 2.74 us
  Pallas kernels: 0 us -> 18.7 us
  other arithmetic: 11.7 us -> 1.87 us
    all_gather x4 -> x0, blocking collectives: 109 us -> none  [the longest x2 61.1 us: joined(): pieces = jax.tree.map(lambda part: lax.all_gather(part, axis), value)]
    psum x1, waiting for transfers between devices: 0.01 us -> 76.5 us  [body(): anchor = lax.psum(jnp.where(mine, prefix_kv[:, 0], 0).astype(BF16), 'ctx')]
    another operation x4 -> x0, loops' own time: 46.2 us -> none  [the longest x1 42.1 us: body(): lax.map(one_head, (head_queries, jnp.arange(head_count, dtype=jnp.int32)))]
    dot_general x36 -> x0, matrix products: 28.4 us -> none  [the longest x18 21.2 us: attend(): jnp.einsum('rgd,kd->rgk', queries, key_rows, preferred_element_type=jnp.f...]
    pallas_call x0 -> x1, Pallas kernels: none -> 18.7 us  [body(): pl.pallas_call(functools.partial(kernel, n), out_shape=(jax.ShapeDtypeStr...]
    dynamic_slice x24 -> x0, local copies, waits for them, and re-layouts: 13.3 us -> none  [the longest x16 9.38 us: body(): lax.map(one_head, (head_queries, jnp.arange(head_count, dtype=jnp.int32)))]
    unnamed x1 -> x0, blocking collectives: 13.1 us -> none
    reduce_sum x17 -> x0, other arithmetic: 6.65 us -> none  [attend(): weight_sum = jnp.sum(weights, axis=-1)]
  transfers between devices with their start and end apart: 2 -> 1, of which waited for: 0 -> 1; matrix products, arithmetic and copies ran while one was open for 22% -> 0% of each run, Pallas kernels for 0% -> 0%
where the time goes in v1:
time: 116 us; the launch traced here: 115 us
  waiting for transfers between devices  76.5 us (66%)
  Pallas kernels  18.7 us (16%)
  between operations  15.5 us (13%)
  local copies, waits for them, and re-layouts  2.74 us (2%)
  other arithmetic  1.87 us (2%)
    psum x1, waiting for transfers between devices, body(): anchor = lax.psum(jnp.where(mine, prefix_kv[:, 0], 0).astype(BF16), 'ctx')  76.5 us
    pallas_call x1, Pallas kernels, body(): pl.pallas_call(functools.partial(kernel, n), out_shape=(jax.ShapeDtypeStr...  18.7 us
  transfers between devices with their start and end apart: 1, of which 1 were waited for; matrix products, arithmetic and copies ran while one was open for 0% of the time, Pallas kernels for 0%

profile of v1, /device:TPU:0, one launch (start us, length us, event | category | flops | bytes accessed | tf_op | source)
XLA Modules:
  0.0 115.3 jit_solution(382470721191699023)
XLA Ops:
  7.2 0.0 copy-start
  7.2 0.0 all-reduce.2.cloned.1.call-start
  7.9 1.9 %fusion = bf16[2,512,256]{2,1,0:T(8,128)(2,1)} fusion(bf16[2,1,512,256]{3,2,1,0:T(8,128)(2,1)} %param.11, pred[]{:T(512)S(6)} %eq.3), kind=kLoop, calls=%fused_computation.1 | loop fusion | flops 262144 | bytes 1048577 | tf_op jit(solution)/shard_map/jit(_where)/select_n | solution.py:191
  9.8 0.0 copy-start.3
  9.8 0.0 copy-start.2
  9.8 0.0 all-reduce.2.cloned.1.call-update
  9.9 0.0 copy-start.4
  10.6 0.0 copy-done.4
  10.6 0.1 copy.11.pos_ref
  10.7 0.0 copy-done.3
  10.7 76.5 %all-reduce.2.cloned.1.call-done.anchor_ref = bf16[2,512,256]{2,1,0:T(8,128)(2,1)} async-done(((bf16[2,512,256]{2,1,0:T(8,128)(2,1)}), bf16[2,512,256]{2,1,0:T(8,128)(2,1)}) %all-reduce.2.cloned.1.call-update) | async-done | bytes 524304 | tf_op jit(solution)/shard_map/psum | solution.py:191
  87.1 0.0 copy-done
  87.1 0.0 copy-done.2
  87.1 0.0 copy-start.1
  87.2 1.0 copy-done.1
  88.2 18.7 %star_attention.1 = (bf16[256,2048]{1,0:T(8,128)(2,1)S(1)}, bf16[32,128]{1,0:T(8,128)(2,1)S(1)}) custom-call(s32[1]{0:T(128)S(6)} %copy.18.len_ref, s32[2,1]{1,0:T(2,128)S(1)} %copy.11.pos_ref, bf16[256,2048]{1,0:T(8,128)(2,1)S(1)} %copy-done, bf16[2,256,256]{2,1,0:T(8,128)(2,1)S(1)} %copy-done.2, bf16[2,512,256]{2,1,0:T(8,128)(2,1)S(1)} %copy-done.1, ...), custom_call_target="tpu_custom_call" | custom-call | flops 1610612736 | bytes 2097152 | tf_op jit(solution)/shard_map/star_attention/pallas_call | solution.py:197
  106.9 0.6 reshape.22
  107.5 1.0 copy.20
  (3 shorter events, 0.0 us)
Async XLA Ops:
  7.2 80.0 %copy-start = (bf16[256,2048]{1,0:T(8,128)(2,1)S(1)}, bf16[256,2048]{1,0:T(8,128)(2,1)}, u32[]{:S(2)}) copy-start(bf16[256,2048]{1,0:T(8,128)(2,1)} %q_ref.1) | copy-start | bytes 3145732
  7.2 80.0 %all-reduce.2.cloned.1.call-start = ((), (), s32[]{:S(2)}) async-start(), calls=%async_computation | async-start | bytes 1048576 | tf_op jit(solution)/shard_map/psum | solution.py:191
  9.8 0.8 copy-start.3
  9.8 77.3 %copy-start.2 = (bf16[2,256,256]{2,1,0:T(8,128)(2,1)S(1)}, bf16[2,256,256]{2,1,0:T(8,128)(2,1)}, u32[]{:S(2)}) copy-start(bf16[2,256,256]{2,1,0:T(8,128)(2,1)} %kv_ref.1) | copy-start | bytes 786436
  9.9 0.7 copy-start.4
  87.1 1.0 copy-start.1
Sparse Core Ops, SparseCore 0:
  12.0 75.0 all-reduce.1

commit v2 on v1

--- a/solution.py
+++ b/solution.py
@@ -32,12 +32,19 @@
 
 
 def kernel(
-    n, len_ref, pos_ref, q_ref, kv_ref, anchor_ref, dq_ref, out_ref, dout_ref,
-    qall, info, psend, precv, q_send, q_recv, i_send, i_recv, p_send, p_recv,
+    n, len_ref, pos_ref, tenant_ref, q_ref, kv_ref, prefix_ref, dq_ref, out_ref, dout_ref,
+    qall, info, psend, precv, y_in, z_out, z_in, anchor,
+    q_send, q_recv, i_send, i_recv, p_send, p_recv,
+    y_send, y_recv, zr_send, zr_recv, za_send, za_recv, yb_send, yb_recv,
 ):
     me = lax.axis_index("ctx")
+    zs = n // 2
+    my_y, my_z = lax.rem(me, 2), me // 2
+    partner = my_z * 2 + 1 - my_y
+    tenant = tenant_ref[0]
     rows, width = q_ref.shape
-    anc = anchor_ref.shape[1]
+    anc = prefix_ref.shape[2]
+    piece = anc // zs
     groups = kv_ref.shape[2] // HD
     per_group = width // HD // groups
     steps = pos_ref.shape[0]
@@ -64,6 +71,69 @@
             send_sem=p_send.at[peer], recv_sem=p_recv.at[source],
             device_id={"ctx": peer}, device_id_type=pl.DeviceIdType.MESH,
         )
+
+    def copy_to(src, dst, send, recv, peer):
+        return pltpu.make_async_remote_copy(
+            src_ref=src, dst_ref=dst, send_sem=send, recv_sem=recv,
+            device_id={"ctx": peer}, device_id_type=pl.DeviceIdType.MESH,
+        )
+
+    def pieces(z):
+        return pl.ds(pl.multiple_of(z * piece, piece), piece)
+
+    def half_out(g):
+        return copy_to(
+            prefix_ref.at[1 - my_y, 0, :, g * HD:(g + 1) * HD], y_in.at[g],
+            y_send.at[g], y_recv.at[g], partner)
+
+    def piece_out(g, z, source):
+        return copy_to(
+            z_out.at[g, pieces(z)], z_in[g].at[source],
+            zr_send.at[g, z], zr_recv.at[g, source], z * 2 + my_y)
+
+    def chosen_out(g, z, source):
+        rows_ = anchor.at[g, my_y, pieces(source)]
+        return copy_to(
+            rows_, rows_, za_send.at[g, z], za_recv.at[g, source], z * 2 + my_y)
+
+    def half_back(g, half, z):
+        rows_ = anchor.at[g, half, pieces(z)]
+        return copy_to(rows_, rows_, yb_send.at[g, z], yb_recv.at[g, z], partner)
+
+    def line(act):
+        def step(d, carry):
+            act(lax.rem(my_z + d, zs))
+            return carry
+        lax.fori_loop(1, zs, step, 0)
+
+    def scatter(g):
+        half_out(g).wait_recv()
+        held = jnp.full((anc, HD), jnp.where(tenant == me, 1, 0), jnp.int32) > 0
+        own = prefix_ref[my_y, 0, :, g * HD:(g + 1) * HD].astype(F32)
+        z_out[g] = jnp.where(held, own, y_in[g].astype(F32)).astype(BF16)
+        line(lambda z: piece_out(g, z, my_z).start())
+        z_in[g][my_z] = z_out[g, pieces(my_z)]
+
+    def gather(g):
+        line(lambda z: piece_out(g, z, z).wait_recv())
+        anchor[g, my_y, pieces(my_z)] = z_in[g][tenant // 2]
+        line(lambda z: chosen_out(g, z, my_z).start())
+        half_back(g, my_y, my_z).start()
+
+    def hand_back(g):
+        def forward(z):
+            chosen_out(g, z, z).wait_recv()
+            half_back(g, my_y, z).start()
+        line(forward)
+
+    def arrive(g):
+        lax.fori_loop(0, zs, lambda z, c: (half_back(g, 1 - my_y, z).wait_recv(), c)[1], 0)
+
+    def finish(g):
+        half_out(g).wait_send()
+        line(lambda z: piece_out(g, z, my_z).wait_send())
+        line(lambda z: chosen_out(g, z, my_z).wait_send())
+        lax.fori_loop(0, zs, lambda z, c: (half_back(g, my_y, z).wait_send(), c)[1], 0)
 
     def peers(act):
         def step(d, carry):
@@ -84,7 +154,10 @@
         for copy in query_copies(peer, me):
             copy.start()
 
+    half_out(0).start()
     peers(send_queries)
+    for g in range(1, groups):
+        half_out(g).start()
 
     row_index = lax.broadcasted_iota(jnp.int32, (rows, rows), 0)
     key_index = lax.broadcasted_iota(jnp.int32, (rows, rows), 1)
@@ -94,28 +167,31 @@
     def prefill_group(g):
         lanes = slice(g * HD, (g + 1) * HD)
 
-        def head(i, carry):
+        def one(i):
             column = pl.ds(pl.multiple_of((g * per_group + i) * HD, HD), HD)
             q = q_ref[:, column]
-            s_a = scores_of(q, anchor_ref[0, :, lanes])
+            s_a = scores_of(q, anchor[g, 0])
             s_b = jnp.where(visible, scores_of(q, kv_ref[0, :, lanes]), MASKED)
             top = jnp.maximum(
                 jnp.max(s_a, axis=1, keepdims=True), jnp.max(s_b, axis=1, keepdims=True))
             w_a = jnp.exp2((s_a - top) * SCALE2)
             w_b = jnp.exp2((s_b - top) * SCALE2)
             weight = jnp.sum(w_a, axis=1, keepdims=True) + jnp.sum(w_b, axis=1, keepdims=True)
-            o = mix(w_a, anchor_ref[1, :, lanes]) + mix(w_b, kv_ref[1, :, lanes])
+            o = mix(w_a, anchor[g, 1]) + mix(w_b, kv_ref[1, :, lanes])
             out_ref[:, column] = jnp.where(kept_row, o * (1.0 / weight), 0.0).astype(BF16)
+
+        def heads(i, carry):
+            one(2 * i)
+            one(2 * i + 1)
             return carry
 
-        lax.fori_loop(0, per_group, head, 0)
-
-    prefill_group(0)
+        lax.fori_loop(0, per_group // 2, heads, 0)
 
     def wait_queries(peer):
         for copy in query_copies(peer, peer):
             copy.wait_recv()
 
+    scatter(0)
     peers(wait_queries)
 
     def add_length(source, sum_):
@@ -143,19 +219,25 @@
     peers(lambda peer: partial_copy(peer, me).start())
 
     for g in range(1, groups):
+        scatter(g)
+    for g in range(groups):
+        gather(g)
+    for g in range(groups):
+        hand_back(g)
+    for g in range(groups):
+        arrive(g)
         prefill_group(g)
 
     own_limit = info[me, 0:drows]
     own_lane = lax.broadcasted_iota(jnp.int32, (drows, HD), 1)
     anchored = []
     for g in range(groups):
-        lanes = slice(g * HD, (g + 1) * HD)
-        s = scores_of(dq_ref[g * drows:(g + 1) * drows], anchor_ref[0, :, lanes])
+        s = scores_of(dq_ref[g * drows:(g + 1) * drows], anchor[g, 0])
         seen = jnp.concatenate([own_lane + c * HD < own_limit for c in range(anc // HD)], axis=1)
         s = jnp.where(seen, s, MASKED)
         top = jnp.max(s, axis=1, keepdims=True)
         w = jnp.where(seen, jnp.exp2((s - top) * SCALE2), 0.0)
-        anchored.append((top, jnp.sum(w, axis=1, keepdims=True), mix(w, anchor_ref[1, :, lanes])))
+        anchored.append((top, jnp.sum(w, axis=1, keepdims=True), mix(w, anchor[g, 1])))
 
     peers(lambda peer: partial_copy(peer, peer).wait_recv())
     for g in range(groups):
@@ -179,6 +261,8 @@
         partial_copy(peer, me).wait_send()
 
     peers(wait_sends)
+    for g in range(groups):
+        finish(g)
 
 
 def body(n, block_q, block_kv, lengths, tenant, prefix_kv, decode_q, decode_pos):
@@ -187,34 +271,40 @@
     per_group = width // HD // groups
     steps = decode_q.shape[0]
     total = steps * width // HD
-    mine = lax.axis_index("ctx") == tenant[0]
-    anchor = lax.psum(jnp.where(mine, prefix_kv[:, 0], 0).astype(BF16), "ctx")
     dq = decode_q.reshape(steps, groups, per_group, HD).transpose(1, 0, 2, 3).reshape(total, HD)
     vmem = pl.BlockSpec(memory_space=pltpu.VMEM)
     smem = pl.BlockSpec(memory_space=pltpu.SMEM)
     heads = width // HD
-    keys = anchor.shape[1] + rows
+    anc = prefix_kv.shape[2]
+    zs = n // 2
+    keys = anc + rows
     out, dout = pl.pallas_call(
         functools.partial(kernel, n),
         out_shape=(
             jax.ShapeDtypeStruct((rows, width), BF16),
             jax.ShapeDtypeStruct((total, HD), BF16),
         ),
-        in_specs=[smem, smem, vmem, vmem, vmem, vmem],
+        in_specs=[smem, smem, smem, vmem, vmem, vmem, vmem],
         out_specs=(vmem, vmem),
         scratch_shapes=[
             pltpu.VMEM((n, total, HD), BF16),
             pltpu.VMEM((n, steps * per_group + 8, HD), jnp.int32),
             pltpu.VMEM((n, 2 * total, HD), BF16),
             pltpu.VMEM((n, 2 * total, HD), BF16),
-        ] + [pltpu.SemaphoreType.DMA((n,))] * 6,
+            pltpu.VMEM((groups, anc, HD), BF16),
+            pltpu.VMEM((groups, anc, HD), BF16),
+            [pltpu.VMEM((zs, anc // zs, HD), BF16)] * groups,
+            pltpu.VMEM((groups, 2, anc, HD), BF16),
+        ] + [pltpu.SemaphoreType.DMA((n,))] * 6
+        + [pltpu.SemaphoreType.DMA((groups,))] * 2
+        + [pltpu.SemaphoreType.DMA((groups, zs))] * 6,
         compiler_params=pltpu.CompilerParams(
             collective_id=0, has_side_effects=True, vmem_limit_bytes=40 * 1024 * 1024),
         cost_estimate=pl.CostEstimate(
             flops=4 * heads * rows * keys * HD, bytes_accessed=4 * rows * width,
             transcendentals=heads * rows * keys),
         name="star_attention",
-    )(lengths, decode_pos, block_q, block_kv, anchor, dq)
+    )(lengths, decode_pos, tenant, block_q, block_kv, prefix_kv, dq)
     dout = dout.reshape(groups, steps, per_group, HD).transpose(1, 0, 2, 3)
     return out, dout.reshape(steps, 1, width)
 

time: 116 us -> 50.5 us (0.44)
  waiting for transfers between devices: 76.5 us -> 0 us
  Pallas kernels: 18.7 us -> 42 us
  between operations: 15.5 us -> 1.95 us
  local copies, waits for them, and re-layouts: 2.74 us -> 6.24 us
  other arithmetic: 1.87 us -> 0 us
    psum x1 -> x0, waiting for transfers between devices: 76.5 us -> none  [body(): anchor = lax.psum(jnp.where(mine, prefix_kv[:, 0], 0).astype(BF16), 'ctx')]
    pallas_call x1, Pallas kernels: 18.7 us -> 42 us  [body(): pl.pallas_call(functools.partial(kernel, n), out_shape=(jax.ShapeDtypeStr...]
    unnamed x13 -> x11, local copies, waits for them, and re-layouts: 2.13 us -> 5.62 us
    select_n x1 -> x0, other arithmetic: 1.87 us -> none  [body(): anchor = lax.psum(jnp.where(mine, prefix_kv[:, 0], 0).astype(BF16), 'ctx')]
  transfers between devices with their start and end apart: 1 -> 0, of which waited for: 1 -> 0; matrix products, arithmetic and copies ran while one was open for 0% -> 0% of each run, Pallas kernels for 0% -> 0%
where the time goes in v2:
time: 50.5 us; the launch traced here: 50.2 us
  Pallas kernels  42 us (83%)
  local copies, waits for them, and re-layouts  6.24 us (12%)
  between operations  1.95 us (4%)
    pallas_call x1, Pallas kernels, body(): pl.pallas_call(functools.partial(kernel, n), out_shape=(jax.ShapeDtypeStr...  42 us
    unnamed x11, local copies, waits for them, and re-layouts  5.62 us

profile of v2, /device:TPU:0, one launch (start us, length us, event | category | flops | bytes accessed | tf_op | source)
XLA Modules:
  0.0 50.2 jit_solution(9275542753061538986)
XLA Ops:
  1.9 0.0 copy-start.3
  1.9 0.6 %copy-done.3 = s32[2,1]{0,1:T(1,128)S(1)} copy-done((s32[2,1]{0,1:T(1,128)S(1)}, s32[2,1]{0,1:T(1,128)}, u32[]{:S(2)}) %copy-start.3) | copy-done | bytes 32
  2.6 0.1 copy.10.pos_ref
  2.7 0.7 %copy.14 = bf16[1,2,16,128]{3,2,1,0:T(8,128)(2,1)S(1)} copy(bf16[1,2,16,128]{3,1,2,0:T(2,128)(2,1)} %bitcast.18) | data formatting | bytes 16384
  3.4 0.0 copy-start
  3.4 1.2 %copy-done = bf16[256,2048]{1,0:T(8,128)(2,1)S(1)} copy-done((bf16[256,2048]{1,0:T(8,128)(2,1)S(1)}, bf16[256,2048]{1,0:T(8,128)(2,1)}, u32[]{:S(2)}) %copy-start) | copy-done | bytes 1048600
  4.6 0.0 copy-start.1
  4.6 1.0 %copy-done.1 = bf16[2,1,512,256]{3,2,1,0:T(8,128)(2,1)S(1)} copy-done((bf16[2,1,512,256]{3,2,1,0:T(8,128)(2,1)S(1)}, bf16[2,1,512,256]{3,2,1,0:T(8,128)(2,1)}, u32[]{:S(2)}) %copy-start.1) | copy-done | bytes 524312
  5.6 0.0 copy-start.2
  5.6 0.9 %copy-done.2 = bf16[2,256,256]{2,1,0:T(8,128)(2,1)S(1)} copy-done((bf16[2,256,256]{2,1,0:T(8,128)(2,1)S(1)}, bf16[2,256,256]{2,1,0:T(8,128)(2,1)}, u32[]{:S(2)}) %copy-start.2) | copy-done | bytes 262168
  6.6 42.0 %star_attention.1 = (bf16[256,2048]{1,0:T(8,128)(2,1)S(1)}, bf16[32,128]{1,0:T(8,128)(2,1)S(1)}) custom-call(s32[1]{0:T(128)S(6)} %copy.16.len_ref, s32[2,1]{1,0:T(2,128)S(1)} %copy.10.pos_ref, s32[1]{0:T(128)S(6)} %copy.17.tenant_ref, bf16[256,2048]{1,0:T(8,128)(2,1)S(1)} %copy-done, bf16[2,256,256]{2,1,0:T(8,128)(2,1)S(1)} %copy-done.2, ...), custom_call_target="tpu_custom_call" | custom-call | flops 1610612736 | bytes 2097152 | tf_op jit(solution)/shard_map/star_attention/pallas_call | solution.py:281
  48.6 0.6 %reshape.19 = bf16[2,1,2048]{2,0,1:T(2,128)(2,1)} reshape(bf16[2,2,8,128]{3,2,1,0:T(8,128)(2,1)S(1)} %copy.11) | data formatting | bytes 16384 | tf_op jit(solution)/shard_map/reshape | solution.py:309
  49.2 1.0 %copy.18 = bf16[256,2048]{1,0:T(8,128)(2,1)} copy(bf16[256,2048]{1,0:T(8,128)(2,1)S(1)} %get-tuple-element.8) | data formatting | bytes 2097152
  (2 shorter events, 0.0 us)
Async XLA Ops:
  1.9 0.7 %copy-start.3 = (s32[2,1]{0,1:T(1,128)S(1)}, s32[2,1]{0,1:T(1,128)}, u32[]{:S(2)}) copy-start(s32[2,1]{0,1:T(1,128)} %param.13) | copy-start | bytes 28
  3.4 1.2 %copy-start = (bf16[256,2048]{1,0:T(8,128)(2,1)S(1)}, bf16[256,2048]{1,0:T(8,128)(2,1)}, u32[]{:S(2)}) copy-start(bf16[256,2048]{1,0:T(8,128)(2,1)} %q_ref.1) | copy-start | bytes 3145732
  4.6 1.0 %copy-start.1 = (bf16[2,1,512,256]{3,2,1,0:T(8,128)(2,1)S(1)}, bf16[2,1,512,256]{3,2,1,0:T(8,128)(2,1)}, u32[]{:S(2)}) copy-start(bf16[2,1,512,256]{3,2,1,0:T(8,128)(2,1)} %prefix_ref.1) | copy-start | bytes 1572868
  5.6 0.9 %copy-start.2 = (bf16[2,256,256]{2,1,0:T(8,128)(2,1)S(1)}, bf16[2,256,256]{2,1,0:T(8,128)(2,1)}, u32[]{:S(2)}) copy-start(bf16[2,256,256]{2,1,0:T(8,128)(2,1)} %kv_ref.1) | copy-start | bytes 786436
